TPU v7x, 768 devices: a whole 4x8x12 slice. The times are simulated.
768 devices in a mesh: dp: 96 (over y, z), head: 4 (over x_lo, core), sub: 2 (over x_hi).
Axes of the slice: x: 4 (x_hi: 2, x_lo: 2; x = x_hi * 2 + x_lo), y: 8, z: 12, core: 2. Of those that a mesh axis runs over, the one named last changes fastest.
Arguments:
- queries: bfloat16 [2, 49152, 4096], P('sub', 'dp', 'head'), may hold values from -6 to 6
- key_states: bfloat16 [49152, 1024], P('dp', 'head'), may hold values from -6 to 6
- value_states: bfloat16 [49152, 1024], P('dp', 'head'), may hold values from -6 to 6
- out_grad: bfloat16 [2, 49152, 4096], P('sub', 'dp', 'head'), may hold values from -6 to 6
- seg_ids: int32 [49152], P('dp'), may hold values from -1 to 7, as said below
- handed: int32 [96], replicated, may hold values from 0 to 256, as said below
Outputs:
- attended: bfloat16 [2, 49152, 4096], P('sub', 'dp', 'head')
- query_grad: bfloat16 [2, 49152, 4096], P('sub', 'dp', 'head')
- key_grad: bfloat16 [49152, 1024], P('dp', ('head', 'sub'))
- value_grad: bfloat16 [49152, 1024], P('dp', ('head', 'sub'))
Inputs may be any that keep to these rules, and one draw needn't show every extreme that they name: `seg_ids`: within a block of 512 slots, live slots come first and numbers never fall; slots of one sequence are contiguous; the first 48 blocks are full, and block 0 holds eight sequences. handed[i] for i < 48 is at least 1 and starts a sequence of block i at slot 512 - handed[i]; it is 0 for the other half. Block i + 48 has at most 512 - handed[i] live slots. handed[0] is 256, and block 48 is exactly full after receiving.
All inputs are finite; a program needn't handle non-finite values.
Results may differ from a plain program's by a relative error of at most 0.022.
Values may be sent and summed in bfloat16 or wider, within the bound.
A program may use at most 32 MiB of HBM per device.

v0:
```python
import jax
import jax.numpy as jnp
from jax import lax
from jax.sharding import PartitionSpec as P

HD = 128


masked_value = -1e30


def passed_along(block, axis, distance):
    devices = range(lax.axis_size(axis))
    route = [(i - distance, i) for i in devices if i - distance in devices]
    return lax.ppermute(block, axis, route)


def placed_rows(own_rows, arrived, kept_count, added_count, filler):
    length = own_rows.shape[0]
    capacity = arrived.shape[0]
    padding = jnp.full((length,) + own_rows.shape[1:], filler, own_rows.dtype)
    widened = jnp.concatenate([padding, arrived, padding], axis=0)
    begin_row = length + capacity - added_count - kept_count
    shifted = lax.dynamic_slice_in_dim(widened, begin_row, length, 0)
    row_index = jnp.arange(length, dtype=jnp.int32).reshape((length,) + (1,) * (own_rows.ndim - 1))
    blank = jnp.asarray(filler, own_rows.dtype)
    return jnp.where(
        row_index < kept_count,
        own_rows,
        jnp.where(row_index < kept_count + added_count, shifted, blank),
    )


def attend(query_heads, key_heads, value_heads, grad_heads, segment):
    length, groups, per_group, head_width = query_heads.shape
    scaling = head_width ** (-0.5)
    key_span = min(128, length)
    live_mask = segment >= 0
    live_rows = jnp.sum(live_mask.astype(jnp.int32))
    block_count = (live_rows + key_span - 1) // key_span
    row_index = jnp.arange(length, dtype=jnp.int32)

    def block_scores(begin_row):
        key_block = lax.dynamic_slice_in_dim(key_heads, begin_row, key_span, 0)
        value_block = lax.dynamic_slice_in_dim(value_heads, begin_row, key_span, 0)
        key_segment = lax.dynamic_slice_in_dim(segment, begin_row, key_span, 0)
        key_index = begin_row + jnp.arange(key_span, dtype=jnp.int32)
        allowed = (
            (segment[:, None] == key_segment[None, :])
            & (key_index[None, :] <= row_index[:, None])
            & live_mask[:, None]
        )
        scores = (
            jnp.einsum("tgjd,ugd->gjtu", query_heads, key_block, preferred_element_type=jnp.float32)
            * scaling
        )
        return (jnp.where(allowed, scores, masked_value), allowed, key_block, value_block)

    def max_pass(block_number, state_pair):
        running_max, running_sum = state_pair
        scores, allowed, key_block, value_block = block_scores(block_number * key_span)
        new_max = jnp.maximum(running_max, jnp.max(scores, axis=-1))
        running_sum = running_sum * jnp.exp(running_max - new_max) + jnp.sum(
            jnp.exp(scores - new_max[..., None]), axis=-1
        )
        return (new_max, running_sum)

    start_max = jnp.full((groups, per_group, length), masked_value, jnp.float32)
    running_max, running_sum = lax.fori_loop(
        0, block_count, max_pass, (start_max, jnp.zeros_like(start_max))
    )
    log_total = running_max + jnp.log(running_sum)

    def output_pass(block_number, running_total):
        scores, allowed, key_block, value_block = block_scores(block_number * key_span)
        weights = jnp.where(allowed, jnp.exp(scores - log_total[..., None]), 0.0).astype(
            jnp.bfloat16
        )
        return running_total + jnp.einsum(
            "gjtu,ugd->tgjd", weights, value_block, preferred_element_type=jnp.float32
        )

    attended = lax.fori_loop(
        0, block_count, output_pass, jnp.zeros(query_heads.shape, jnp.float32)
    ).astype(jnp.bfloat16)
    row_delta = jnp.einsum(
        "tgjd,tgjd->gjt", grad_heads, attended, preferred_element_type=jnp.float32
    )

    def grad_pass(block_number, grad_state):
        query_total, key_total, value_total = grad_state
        begin_row = block_number * key_span
        scores, allowed, key_block, value_block = block_scores(begin_row)
        probabilities = jnp.where(allowed, jnp.exp(scores - log_total[..., None]), 0.0)
        weights = probabilities.astype(jnp.bfloat16)
        prob_grad = jnp.einsum(
            "tgjd,ugd->gjtu", grad_heads, value_block, preferred_element_type=jnp.float32
        )
        score_grad = (probabilities * (prob_grad - row_delta[..., None])).astype(jnp.bfloat16)
        query_total = query_total + jnp.einsum(
            "gjtu,ugd->tgjd", score_grad, key_block, preferred_element_type=jnp.float32
        )
        key_part = jnp.einsum(
            "gjtu,tgjd->ugd", score_grad, query_heads, preferred_element_type=jnp.float32
        )
        value_part = jnp.einsum(
            "gjtu,tgjd->ugd", weights, grad_heads, preferred_element_type=jnp.float32
        )
        key_total = lax.dynamic_update_slice_in_dim(key_total, key_part, begin_row, 0)
        value_total = lax.dynamic_update_slice_in_dim(value_total, value_part, begin_row, 0)
        return (query_total, key_total, value_total)

    zero_keys = jnp.zeros(key_heads.shape, jnp.float32)
    query_total, key_total, value_total = lax.fori_loop(
        0, block_count, grad_pass, (jnp.zeros(query_heads.shape, jnp.float32), zero_keys, zero_keys)
    )
    return (
        attended,
        (query_total * scaling).astype(jnp.bfloat16),
        key_total * scaling,
        value_total,
    )


def summed_key_grads(key_total, value_total):
    length = key_total.shape[0]
    summed = (
        lax.psum_scatter(key_total.reshape(length, -1), "sub", scatter_dimension=1, tiled=True),
        lax.psum_scatter(value_total.reshape(length, -1), "sub", scatter_dimension=1, tiled=True),
    )
    return (summed[0].astype(jnp.bfloat16), summed[1].astype(jnp.bfloat16))


def on_device(queries, key_states, value_states, out_grad, seg_ids, handed):
    length = seg_ids.shape[0]
    capacity = length // 2
    tail_start = length - capacity
    groups = key_states.shape[1] // HD
    query_rows = queries[0]
    grad_rows = out_grad[0]
    row_width = query_rows.shape[1]
    position = lax.axis_index("dp")
    halfway = lax.axis_size("dp") // 2
    sender = position < halfway
    own_moved = lax.dynamic_index_in_dim(handed, position, 0, keepdims=False)
    partner_moved = lax.dynamic_index_in_dim(
        handed, jnp.maximum(position - halfway, 0), 0, keepdims=False
    )
    own_live = jnp.sum((seg_ids >= 0).astype(jnp.int32))
    kept_count = jnp.where(sender, length - own_moved, own_live)
    added_count = jnp.where(sender, 0, partner_moved)

    def as_heads(flat_rows):
        return flat_rows.reshape(length, groups, -1, HD)

    def as_keys(flat_rows):
        return flat_rows.reshape(length, groups, HD)

    attended, query_grad, key_total, value_total = attend(
        as_heads(query_rows),
        as_keys(key_states),
        as_keys(value_states),
        as_heads(grad_rows),
        seg_ids,
    )
    key_grad, value_grad = summed_key_grads(key_total, value_total)
    attended = attended.reshape(length, row_width)
    query_grad = query_grad.reshape(length, row_width)
    arrived = passed_along(
        (
            attended[tail_start:],
            query_grad[tail_start:],
            key_grad[tail_start:],
            value_grad[tail_start:],
        ),
        "dp",
        halfway,
    )
    attended = placed_rows(attended, arrived[0], kept_count, added_count, 0.0)
    query_grad = placed_rows(query_grad, arrived[1], kept_count, added_count, 0.0)
    key_grad = placed_rows(key_grad, arrived[2], kept_count, added_count, 0.0)
    value_grad = placed_rows(value_grad, arrived[3], kept_count, added_count, 0.0)
    return (
        attended.reshape(1, length, row_width),
        query_grad.reshape(1, length, row_width),
        key_grad,
        value_grad,
    )


def solution(mesh):
    return jax.shard_map(
        on_device,
        mesh=mesh,
        in_specs=(
            P("sub", "dp", "head"),
            P("dp", "head"),
            P("dp", "head"),
            P("sub", "dp", "head"),
            P("dp"),
            P(),
        ),
        out_specs=(
            P("sub", "dp", "head"),
            P("sub", "dp", "head"),
            P("dp", ("head", "sub")),
            P("dp", ("head", "sub")),
        ),
        check_vma=False,
    )
```

profile of v0, /device:TPU:1, one launch (start us, length us, event | category | flops | bytes accessed | tf_op | source)
XLA Modules:
  0.0 168.0 jit_solution(13504872065480120921)
XLA Ops:
  9.2 1.5 copy.25
  11.4 1.5 copy.29
  14.0 1.5 copy.32
  16.3 5.2 %while.39 = (s32[]{:T(128)}, f32[2,4,512]{2,1,0:T(4,128)S(1)}, f32[2,4,512]{2,1,0:T(4,128)S(1)}, s32[]{:T(128)}, s32[512]{0:T(512)S(1)}, /*index=5*/pred[512]{0:...) while((s32[]{:T(128)}, f32[2,4,512]{2,1,0:T(4,128)S(1)}, ...), condition=%wide.region_4.5_spmd.clone, body=%wide.region_1.4_spmd.clone.sunk | while | flops 138158208 | bytes 5723311 | solution.py:69
  22.1 1.6 broadcast.67.clone
  23.7 25.2 %while.40 = (s32[]{:T(128)}, f32[512,2,4,128]{0,3,2,1:T(8,128)}, s32[]{:T(128)}, bf16[512,2,128]{0,2,1:T(8,128)(2,1)}, s32[512]{0:T(512)S(1)}, /*index=5*/pred[5...) while((s32[]{:T(128)}, f32[512,2,4,128]{0,3,2,1:T(8,128)}, ...), condition=%wide.region_6.7_spmd.clone, body=%wide.region_5.6_spmd.clone.sunk | while | flops 271843456 | bytes 5788859 | solution.py:83
  25.6 4.4 %bitcast_add_fusion.4 = f32[512,2,4,128]{0,3,2,1:T(8,128)} fusion(f32[512,2,4,128]{0,3,2,1:T(8,128)} %get-tuple-element.609, bf16[512,2,4,128]{3,2,1,0:T(4,128)(2,1)} %get-tuple-element.628, f32[2,4,512]{2,1,0:T(4,128)} %get-tuple-element.629, pred[512,128]{1,0:T(8,128)(4,1)S(1)} %fusion.106, bf16[128,2,128,1]{2,1,0,3:T(2,128)(2,1)} %bitcast.189, ...), kind=kOutput, calls=%fused_computation.15.clone.1 | convolution fusion | flops 271581184 | bytes 5455876 | tf_op jit(solution)/shard_map/while/body/gjtu,ugd->tgjd/dot_general | solution.py:79
  31.9 4.4 %bitcast_add_fusion.4 = f32[512,2,4,128]{0,3,2,1:T(8,128)} fusion(f32[512,2,4,128]{0,3,2,1:T(8,128)} %get-tuple-element.609, bf16[512,2,4,128]{3,2,1,0:T(4,128)(2,1)} %get-tuple-element.628, f32[2,4,512]{2,1,0:T(4,128)} %get-tuple-element.629, pred[512,128]{1,0:T(8,128)(4,1)S(1)} %fusion.106, bf16[128,2,128,1]{2,1,0,3:T(2,128)(2,1)} %bitcast.189, ...), kind=kOutput, calls=%fused_computation.15.clone.1 | convolution fusion | flops 271581184 | bytes 5455876 | tf_op jit(solution)/shard_map/while/body/gjtu,ugd->tgjd/dot_general | solution.py:79
  38.1 4.4 %bitcast_add_fusion.4 = f32[512,2,4,128]{0,3,2,1:T(8,128)} fusion(f32[512,2,4,128]{0,3,2,1:T(8,128)} %get-tuple-element.609, bf16[512,2,4,128]{3,2,1,0:T(4,128)(2,1)} %get-tuple-element.628, f32[2,4,512]{2,1,0:T(4,128)} %get-tuple-element.629, pred[512,128]{1,0:T(8,128)(4,1)S(1)} %fusion.106, bf16[128,2,128,1]{2,1,0,3:T(2,128)(2,1)} %bitcast.189, ...), kind=kOutput, calls=%fused_computation.15.clone.1 | convolution fusion | flops 271581184 | bytes 5455876 | tf_op jit(solution)/shard_map/while/body/gjtu,ugd->tgjd/dot_general | solution.py:79
  44.4 4.4 %bitcast_add_fusion.4 = f32[512,2,4,128]{0,3,2,1:T(8,128)} fusion(f32[512,2,4,128]{0,3,2,1:T(8,128)} %get-tuple-element.609, bf16[512,2,4,128]{3,2,1,0:T(4,128)(2,1)} %get-tuple-element.628, f32[2,4,512]{2,1,0:T(4,128)} %get-tuple-element.629, pred[512,128]{1,0:T(8,128)(4,1)S(1)} %fusion.106, bf16[128,2,128,1]{2,1,0,3:T(2,128)(2,1)} %bitcast.189, ...), kind=kOutput, calls=%fused_computation.15.clone.1 | convolution fusion | flops 271581184 | bytes 5455876 | tf_op jit(solution)/shard_map/while/body/gjtu,ugd->tgjd/dot_general | solution.py:79
  48.8 2.9 %fusion.52 = (f32[2,4,512]{2,1,0:T(4,128)S(1)}, bf16[512,2,4,128]{0,3,2,1:T(8,128)(2,1)}) fusion(bf16[2,4,512,128]{2,3,1,0:T(8,128)(2,1)S(1)} %bitcast.177, f32[512,2,4,128]{0,3,2,1:T(8,128)} %get-tuple-element.183), kind=kLoop, calls=%fused_computation.70 | loop fusion | flops 2617344 | bytes 4210688 | tf_op jit(solution)/shard_map/tgjd,tgjd->gjt/dot_general | solution.py:86
  53.5 1.6 broadcast.67
  55.1 26.8 %while.41 = (s32[]{:T(128)}, f32[512,2,4,128]{0,3,2,1:T(8,128)}, f32[512,2,128]{2,0,1:T(8,128)}, f32[512,2,128]{2,1,0:T(2,128)}, s32[]{:T(128)}, /*index=5*/bf16...) while((s32[]{:T(128)}, f32[512,2,4,128]{0,3,2,1:T(8,128)}, ...), condition=%wide.region_8.9_spmd.clone, body=%wide.region_7.8_spmd.clone.sunk | while | flops 676069504 | bytes 35493148 | solution.py:114
  81.9 2.0 %copy.80 = f32[64,8,2,128]{3,1,2,0:T(8,128)} copy(f32[64,8,2,128]{3,2,1,0:T(2,128)} %bitcast.49) | data formatting | bytes 1048576
  84.0 2.0 %copy_bitcast_fusion.1 = f32[512,256]{1,0:T(8,128)} fusion(f32[512,2,128]{2,0,1:T(8,128)} %get-tuple-element.185), kind=kLoop, calls=%fused_computation.83 | loop fusion | flops 131072 | bytes 1048576 | tf_op jit(solution)/shard_map/reshape | solution.py:128
  86.9 2.0 %copy.58 = bf16[256,1024]{1,0:T(8,128)(2,1)} copy(bf16[256,1024]{0,1:T(8,128)(2,1)} %bitcast.186) | data formatting | bytes 1048576 | tf_op jit(solution)/shard_map/slice | solution.py:171
  88.9 2.1 %collective-permute-start = (bf16[256,1024]{1,0:T(8,128)(2,1)}, bf16[256,1024]{1,0:T(8,128)(2,1)}, u32[]{:S(2)}, u32[]{:S(2)}) collective-permute-start(bf16[256,1024]{1,0:T(8,128)(2,1)} %copy.58), channel_id=1, source_target_pairs={{0,384},{8,392},{16,400},{24,408},{32,416},{40,424},{48,432},{56,4... | collective-permute-start | bytes 1572872 | tf_op jit(solution)/shard_map/ppermute | solution.py:15
  92.3 2.1 %collective-permute-start.1 = (bf16[256,1024]{1,0:T(8,128)(2,1)}, bf16[256,1024]{1,0:T(8,128)(2,1)}, u32[]{:S(2)}, u32[]{:S(2)}) collective-permute-start(bf16[256,1024]{1,0:T(8,128)(2,1)} %copy.62), channel_id=1, source_target_pairs={{0,384},{8,392},{16,400},{24,408},{32,416},{40,424},{48,432},{56,4... | collective-permute-start | bytes 1572872 | tf_op jit(solution)/shard_map/ppermute | solution.py:15
  98.0 18.0 %reduce-scatter.5.cloned.1.call-done = f32[512,128]{1,0:T(8,128)} async-done(((f32[512,256]{1,0:T(8,128)}), f32[512,128]{1,0:T(8,128)}) %reduce-scatter.5.cloned.1.call-update) | async-done | bytes 262160 | tf_op jit(solution)/shard_map/reduce_scatter | solution.py:129
  117.0 7.1 %collective-permute-start.3 = (bf16[256,128]{1,0:T(8,128)(2,1)S(1)}, bf16[256,128]{1,0:T(8,128)(2,1)S(1)}, u32[]{:S(2)}, u32[]{:S(2)}) collective-permute-start(bf16[256,128]{1,0:T(8,128)(2,1)S(1)} %slice.27), channel_id=1, source_target_pairs={{0,384},{8,392},{16,400},{24,408},{32,416},{40,424},{48,432},{56,4... | collective-permute-start | bytes 196616 | tf_op jit(solution)/shard_map/ppermute | solution.py:15
  124.1 21.5 %reduce-scatter.3.cloned.1.call-done = f32[512,128]{1,0:T(8,128)} async-done(((f32[512,256]{1,0:T(8,128)}), f32[512,128]{1,0:T(8,128)}) %reduce-scatter.3.cloned.1.call-update) | async-done | bytes 262160 | tf_op jit(solution)/shard_map/reduce_scatter | solution.py:128
  146.6 7.3 %collective-permute-start.2 = (bf16[256,128]{1,0:T(8,128)(2,1)S(1)}, bf16[256,128]{1,0:T(8,128)(2,1)S(1)}, u32[]{:S(2)}, u32[]{:S(2)}) collective-permute-start(bf16[256,128]{1,0:T(8,128)(2,1)S(1)} %slice.26), channel_id=1, source_target_pairs={{0,384},{8,392},{16,400},{24,408},{32,416},{40,424},{48,432},{56,4... | collective-permute-start | bytes 196616 | tf_op jit(solution)/shard_map/ppermute | solution.py:15
  154.1 5.5 %fusion.62 = (bf16[1,512,1024]{2,1,0:T(8,128)(2,1)}, bf16[1,512,1024]{2,1,0:T(8,128)(2,1)}) fusion(bf16[512,1024]{1,0:T(8,128)(2,1)S(1)} %copy.61, bf16[512,1024]{1,0:T(8,128)(2,1)S(1)} %broadcast.68, s32[]{:T(128)S(6)} %select_n.87, bf16[256,1024]{1,0:T(8,128)(2,1)} %collective-permute-done.1, pred[512]{0:T(512)(128)(4,1)S(1)} %get-tuple-element.367, ...), kind=kLoop, calls=%fused_computation.81 | loop fusion | flops 8388608 | bytes 6292484 | tf_op jit(solution)/shard_map/reshape | solution.py:185
  159.6 1.5 fusion.70
  (159 shorter events, 51.3 us)
Async XLA Ops:
  7.2 108.9 %reduce-scatter.5.cloned.1.call-start = ((), (), s32[]{:S(2)}) async-start(), calls=%async_computation.3 | async-start | bytes 786432 | tf_op jit(solution)/shard_map/reduce_scatter | solution.py:129
  10.7 2.2 %copy-start.9 = (bf16[512,256]{1,0:T(8,128)(2,1)S(1)}, bf16[512,256]{1,0:T(8,128)(2,1)}, u32[]{:S(2)}) copy-start(bf16[512,256]{1,0:T(8,128)(2,1)} %param.13) | copy-start | bytes 786436
  11.4 1.8 %copy-start.10 = (bf16[512,256]{1,0:T(8,128)(2,1)S(1)}, bf16[512,256]{1,0:T(8,128)(2,1)}, u32[]{:S(2)}) copy-start(bf16[512,256]{1,0:T(8,128)(2,1)} %param.14) | copy-start | bytes 786436
  13.0 2.6 %copy-start.5 = (bf16[512,256]{0,1:T(8,128)(2,1)}, bf16[512,256]{0,1:T(8,128)(2,1)S(1)}, u32[]{:S(2)}) copy-start(bf16[512,256]{0,1:T(8,128)(2,1)S(1)} %copy.24) | copy-start | bytes 786436
  14.0 2.2 %copy-start.8 = (s32[512]{0:T(512)S(1)}, s32[512]{0:T(512)}, u32[]{:S(2)}) copy-start(s32[512]{0:T(512)} %param.16) | copy-start | bytes 6148
  51.8 3.4 %copy-start.11 = (f32[2,4,512]{2,1,0:T(4,128)S(1)}, f32[2,4,512]{2,1,0:T(4,128)}, u32[]{:S(2)}) copy-start(f32[2,4,512]{2,1,0:T(4,128)} %get-tuple-element.704) | copy-start | bytes 49156
  57.9 1.9 %copy-start = (f32[512,2,4,128]{0,3,2,1:T(8,128)S(1)}, f32[512,2,4,128]{0,3,2,1:T(8,128)}, u32[]{:S(2)}) copy-start(f32[512,2,4,128]{0,3,2,1:T(8,128)} %get-tuple-element.652) | copy-start | bytes 6291460 | tf_op jit(solution)/shard_map/while
  60.5 1.3 copy-start.1
  64.6 1.9 %copy-start = (f32[512,2,4,128]{0,3,2,1:T(8,128)S(1)}, f32[512,2,4,128]{0,3,2,1:T(8,128)}, u32[]{:S(2)}) copy-start(f32[512,2,4,128]{0,3,2,1:T(8,128)} %get-tuple-element.652) | copy-start | bytes 6291460 | tf_op jit(solution)/shard_map/while
  67.2 1.3 copy-start.1
  71.3 1.9 %copy-start = (f32[512,2,4,128]{0,3,2,1:T(8,128)S(1)}, f32[512,2,4,128]{0,3,2,1:T(8,128)}, u32[]{:S(2)}) copy-start(f32[512,2,4,128]{0,3,2,1:T(8,128)} %get-tuple-element.652) | copy-start | bytes 6291460 | tf_op jit(solution)/shard_map/while
  78.0 1.9 %copy-start = (f32[512,2,4,128]{0,3,2,1:T(8,128)S(1)}, f32[512,2,4,128]{0,3,2,1:T(8,128)}, u32[]{:S(2)}) copy-start(f32[512,2,4,128]{0,3,2,1:T(8,128)} %get-tuple-element.652) | copy-start | bytes 6291460 | tf_op jit(solution)/shard_map/while
  80.6 1.3 copy-start.1
  81.9 4.1 %copy-start.3 = (bf16[512,2,4,128]{0,3,2,1:T(8,128)(2,1)S(1)}, bf16[512,2,4,128]{0,3,2,1:T(8,128)(2,1)}, u32[]{:S(2)}) copy-start(bf16[512,2,4,128]{0,3,2,1:T(8,128)(2,1)} %get-tuple-element.356) | copy-start | bytes 3145732
  83.9 7.1 %copy-start.2 = (f32[512,2,4,128]{0,3,2,1:T(8,128)S(1)}, f32[512,2,4,128]{0,3,2,1:T(8,128)}, u32[]{:S(2)}) copy-start(f32[512,2,4,128]{0,3,2,1:T(8,128)} %get-tuple-element.184) | copy-start | bytes 6291460
  83.9 61.7 %reduce-scatter.3.cloned.1.call-start = ((), (), s32[]{:S(2)}) async-start(), calls=%async_computation.2 | async-start | bytes 786432 | tf_op jit(solution)/shard_map/reduce_scatter | solution.py:128
  88.9 65.0 %collective-permute-start = (bf16[256,1024]{1,0:T(8,128)(2,1)}, bf16[256,1024]{1,0:T(8,128)(2,1)}, u32[]{:S(2)}, u32[]{:S(2)}) collective-permute-start(bf16[256,1024]{1,0:T(8,128)(2,1)} %copy.58), channel_id=1, source_target_pairs={{0,384},{8,392},{16,400},{24,408},{32,416},{40,424},{48,432},{56,4... | collective-permute-start | bytes 1572872 | tf_op jit(solution)/shard_map/ppermute | solution.py:15
  91.0 3.4 %copy-start.12 = (s32[96]{0:T(128)S(1)}, s32[96]{0:T(128)}, u32[]{:S(2)}) copy-start(s32[96]{0:T(128)} %param.17) | copy-start | bytes 1156
  91.3 5.6 %copy-start.4 = (bf16[512,2,4,128]{0,3,2,1:T(8,128)(2,1)S(1)}, bf16[512,2,4,128]{0,3,2,1:T(8,128)(2,1)}, u32[]{:S(2)}) copy-start(bf16[512,2,4,128]{0,3,2,1:T(8,128)(2,1)} %get-tuple-element.356) | copy-start | bytes 3145732
  92.3 61.6 %collective-permute-start.1 = (bf16[256,1024]{1,0:T(8,128)(2,1)}, bf16[256,1024]{1,0:T(8,128)(2,1)}, u32[]{:S(2)}, u32[]{:S(2)}) collective-permute-start(bf16[256,1024]{1,0:T(8,128)(2,1)} %copy.62), channel_id=1, source_target_pairs={{0,384},{8,392},{16,400},{24,408},{32,416},{40,424},{48,432},{56,4... | collective-permute-start | bytes 1572872 | tf_op jit(solution)/shard_map/ppermute | solution.py:15
  117.0 42.5 %collective-permute-start.3 = (bf16[256,128]{1,0:T(8,128)(2,1)S(1)}, bf16[256,128]{1,0:T(8,128)(2,1)S(1)}, u32[]{:S(2)}, u32[]{:S(2)}) collective-permute-start(bf16[256,128]{1,0:T(8,128)(2,1)S(1)} %slice.27), channel_id=1, source_target_pairs={{0,384},{8,392},{16,400},{24,408},{32,416},{40,424},{48,432},{56,4... | collective-permute-start | bytes 196616 | tf_op jit(solution)/shard_map/ppermute | solution.py:15
  146.6 12.9 %collective-permute-start.2 = (bf16[256,128]{1,0:T(8,128)(2,1)S(1)}, bf16[256,128]{1,0:T(8,128)(2,1)S(1)}, u32[]{:S(2)}, u32[]{:S(2)}) collective-permute-start(bf16[256,128]{1,0:T(8,128)(2,1)S(1)} %slice.26), channel_id=1, source_target_pairs={{0,384},{8,392},{16,400},{24,408},{32,416},{40,424},{48,432},{56,4... | collective-permute-start | bytes 196616 | tf_op jit(solution)/shard_map/ppermute | solution.py:15
  154.0 5.5 %copy-start.6 = (f32[512,128]{1,0:T(8,128)S(1)}, f32[512,128]{1,0:T(8,128)}, u32[]{:S(2)}) copy-start(f32[512,128]{1,0:T(8,128)} %reduce-scatter.5.cloned.1.call-done) | copy-start | bytes 786436
  154.1 5.5 %copy-start.7 = (f32[512,128]{1,0:T(8,128)S(1)}, f32[512,128]{1,0:T(8,128)}, u32[]{:S(2)}) copy-start(f32[512,128]{1,0:T(8,128)} %reduce-scatter.3.cloned.1.call-done) | copy-start | bytes 786436
  (1 other events, 1.3 us)
Sparse Core Ops, SparseCore 0:
  84.0 31.9 reduce-scatter.4
  119.4 26.1 reduce-scatter.2
where the time goes:
time: 169 us; the launch traced here: 168 us
  waiting for transfers between devices  39.6 us (23%)
  matrix products  37 us (22%)
  local copies, waits for them, and re-layouts  35.4 us (21%)
  other arithmetic  20 us (12%)
  starting transfers between devices  18.6 us (11%)
  between operations  16.9 us (10%)
    reduce_scatter x1, waiting for transfers between devices, summed_key_grads(): lax.psum_scatter(key_total.reshape(length, -1), 'sub', scatter_dimension=...  21.5 us
    ppermute x4, starting transfers between devices, passed_along(): return lax.ppermute(block, axis, route)  18.5 us
    reduce_scatter x1, waiting for transfers between devices, summed_key_grads(): lax.psum_scatter(value_total.reshape(length, -1), 'sub', scatter_dimensio...  18 us
    dot_general x4, matrix products, output_pass(): jnp.einsum('gjtu,ugd->tgjd', weights, value_block, preferred_element_type...  17.6 us
    unnamed x31, local copies, waits for them, and re-layouts  8.97 us
    dynamic_slice x8, local copies, waits for them, and re-layouts, block_scores(): key_block = lax.dynamic_slice_in_dim(key_heads, begin_row, key_span, 0)  6.44 us
    reshape x1, other arithmetic, on_device(): query_grad.reshape(1, length, row_width)  5.49 us
    dot_general x4, matrix products, grad_pass(): jnp.einsum('tgjd,ugd->gjtu', grad_heads, value_block, preferred_element_t...  5.38 us
  transfers between devices with their start and end apart: 6, of which 2 were waited for; matrix products, arithmetic and copies ran while one was open for 9% of the time, Pallas kernels for 0%

commit v1 on v0

v1 whole, which is shorter than its diff:
```python
import functools

import jax
import jax.numpy as jnp
from jax import lax
from jax.experimental import pallas as pl
from jax.experimental.pallas import tpu as pltpu
from jax.sharding import PartitionSpec as P

HD = 128
STEP = 16
PAIRS = 3
FOLDED = STEP * (2 * PAIRS + 1)
LOG2_E = 1.4426950408889634
MASKED = -1e30
MESH = pl.DeviceIdType.MESH


def dot_nn(a, b):
    return lax.dot_general(a, b, (((1,), (0,)), ((), ())), preferred_element_type=jnp.float32)


def dot_nt(a, b):
    return lax.dot_general(a, b, (((1,), (1,)), ((), ())), preferred_element_type=jnp.float32)


def dot_tn(a, b):
    return lax.dot_general(a, b, (((0,), (0,)), ((), ())), preferred_element_type=jnp.float32)


def attention_rows(query, grad, key, value, bias, scaling):
    scores = dot_nt(query, key) * (scaling * LOG2_E) + bias
    raised = jnp.exp2(scores - jnp.max(scores, axis=1, keepdims=True))
    probs = raised * (1.0 / jnp.sum(raised, axis=1, keepdims=True))
    weights = probs.astype(jnp.bfloat16)
    output = dot_nn(weights, value).astype(jnp.bfloat16)
    delta = jnp.sum(grad.astype(jnp.float32) * output.astype(jnp.float32), axis=1, keepdims=True)
    score_grad = probs * (dot_nt(grad, value) - delta)
    rounded = score_grad.astype(jnp.bfloat16)
    query_grad = (dot_nn(rounded, key) * scaling).astype(jnp.bfloat16)
    return output, query_grad, dot_tn(rounded, query), dot_tn(weights, grad), probs, score_grad


def folded_rows(probs, score_grad):
    rows = []
    for square in (probs, score_grad):
        for j in range(PAIRS):
            low = square[STEP * j : STEP * (j + 1)]
            high = square[STEP * (2 * PAIRS - j) : STEP * (2 * PAIRS - j + 1)]
            rows.append(low + pltpu.roll(high, STEP * (j + 1), 1))
    middle = slice(STEP * PAIRS, STEP * (PAIRS + 1))
    rows.append(probs[middle] + pltpu.roll(score_grad[middle], HD // 2, 1))
    return jnp.concatenate(rows, axis=0).astype(jnp.bfloat16)


def unfolded_rows(packed):
    packed = packed.astype(jnp.float32)
    lane = lax.broadcasted_iota(jnp.int32, (STEP, HD), 1)
    last = packed[2 * PAIRS * STEP :]
    squares = []
    for which in range(2):
        low, high = [], []
        for j in range(PAIRS):
            start = (which * PAIRS + j) * STEP
            rows = packed[start : start + STEP]
            low.append(jnp.where(lane < STEP * (j + 1), rows, 0.0))
            turned = pltpu.roll(rows, HD - STEP * (j + 1), 1)
            high.append(jnp.where(lane < STEP * (2 * PAIRS + 1 - j), turned, 0.0))
        turned = pltpu.roll(last, HD // 2, 1) if which else last
        middle = jnp.where(lane < HD // 2, turned, 0.0)
        squares.append(jnp.concatenate(low + [middle] + high[::-1], axis=0).astype(jnp.bfloat16))
    return squares


def kernel(
    n_dp,
    query_in, key_in, value_in, grad_in, seg_ref, handed_ref,
    out_a, out_q, out_k, out_v,
    query_buf, grad_buf, key_buf, value_buf, att_buf, qg_buf, bias_top, bias_tail,
    key_acc, value_acc, perm, tx, rx, kv_rx, part_tx, part_rx, own_kv, kv_tx, kv_grad_rx,
    in_sem, out_sem, tx_send, tx_recv, kv_send, kv_recv, fwd_send, fwd_recv,
    part_send, part_recv, kvg_send, kvg_recv,
):
    length, width = query_in.shape[1], query_in.shape[2]
    heads = width // HD
    groups = key_in.shape[1] // HD
    per_group = heads // groups
    cap = length // 2
    rest = cap - FOLDED
    scaling = HD ** (-0.5)
    half = n_dp // 2
    me = lax.axis_index("dp")
    sub = lax.axis_index("sub")
    other = 1 - sub
    sender = me < half
    receiver = jnp.logical_not(sender)
    partner = {"dp": lax.rem(me + half, n_dp)}
    twin = {"sub": other}

    def columns(h):
        return pl.ds(pl.multiple_of(h * HD, HD), HD)

    def fetch(kind, h, part):
        source = (query_in, grad_in)[kind]
        target = (query_buf, grad_buf)[kind]
        rows = pl.ds(part * cap, cap)
        return pltpu.make_async_copy(
            source.at[0, rows, columns(h)], target.at[h, rows], in_sem.at[(kind * 2 + part) * heads + h]
        )

    def fetch_kv(kind, g):
        source = (key_in, value_in)[kind]
        target = (key_buf, value_buf)[kind]
        return pltpu.make_async_copy(
            source.at[:, columns(g)], target.at[g], in_sem.at[4 * heads + kind * groups + g]
        )

    def remote(source, target, send, recv, to):
        return pltpu.make_async_remote_copy(
            src_ref=source, dst_ref=target, send_sem=send, recv_sem=recv, device_id=to, device_id_type=MESH
        )

    def kv_copy(kind):
        source = (key_buf, value_buf)[kind]
        return remote(
            source.at[sub, pl.ds(cap, FOLDED)], kv_rx.at[kind, sub, pl.ds(0, FOLDED)],
            kv_send.at[kind], kv_recv.at[kind], partner,
        )

    def kv_forward(kind):
        rows = pl.ds(0, FOLDED)
        return remote(
            kv_rx.at[kind, sub, rows], kv_rx.at[kind, sub, rows], fwd_send.at[kind], fwd_recv.at[kind], twin
        )

    def head_copy(h):
        return remote(tx.at[h], rx.at[h], tx_send.at[h], tx_recv.at[h], partner)

    def part_copy(part):
        rows = pl.ds(part * cap, cap)
        return remote(
            part_tx.at[:, rows], part_rx.at[:, rows], part_send.at[part], part_recv.at[part], twin
        )

    def kv_grad_copy():
        return remote(kv_tx, kv_grad_rx, kvg_send.at[0], kvg_recv.at[0], partner)

    for g in range(groups):
        fetch_kv(0, g).start()
        fetch_kv(1, g).start()
    for part in (1, 0):
        for h in range(heads):
            fetch(0, h, part).start()
            fetch(1, h, part).start()

    barrier = pltpu.get_barrier_semaphore()
    pl.semaphore_signal(barrier, inc=1, device_id=partner, device_id_type=MESH)
    pl.semaphore_signal(barrier, inc=1, device_id=twin, device_id_type=MESH)
    for g in range(groups):
        fetch_kv(0, g).wait()
        fetch_kv(1, g).wait()
    pl.semaphore_wait(barrier, 2)

    @pl.when(sender)
    def _():
        kv_copy(0).start()
        kv_copy(1).start()

    seg = seg_ref[...].astype(jnp.float32)
    square = (HD, HD)
    below = lax.broadcasted_iota(jnp.int32, square, 1) <= lax.broadcasted_iota(jnp.int32, square, 0)
    blocks = length // HD
    for a in range(blocks):
        of_query = jnp.transpose(jnp.broadcast_to(seg[a : a + 1], square))
        for b in range(blocks):
            top = a < blocks // 2
            if top and b >= blocks // 2:
                continue
            if b > a:
                tile = jnp.full(square, MASKED, jnp.float32)
            else:
                allowed = of_query == jnp.broadcast_to(seg[b : b + 1], square)
                if a == b:
                    allowed = jnp.logical_and(allowed, below)
                tile = jnp.where(allowed, 0.0, MASKED)
            if top:
                bias_top[a * HD : (a + 1) * HD, b * HD : (b + 1) * HD] = tile
            else:
                begin = (a - blocks // 2) * HD
                bias_tail[begin : begin + HD, b * HD : (b + 1) * HD] = tile
    key_acc[...] = jnp.zeros_like(key_acc)
    value_acc[...] = jnp.zeros_like(value_acc)

    def tail_head(h, carry):
        g = h // per_group
        fetch(0, h, 1).wait()
        fetch(1, h, 1).wait()
        query = query_buf[h, cap:]
        grad = grad_buf[h, cap:]
        output, query_grad, key_part, value_part, probs, score_grad = attention_rows(
            query, grad, key_buf[g], value_buf[g], bias_tail[...], scaling
        )
        att_buf[h, cap:] = output
        qg_buf[h, cap:] = query_grad
        key_acc[g] += key_part
        value_acc[g] += value_part

        @pl.when(sender)
        def _():
            tx[h, :rest] = output[FOLDED:]
            tx[h, rest : 2 * rest] = query_grad[FOLDED:]
            tx[h, 2 * rest :] = folded_rows(probs[:FOLDED, cap : cap + HD], score_grad[:FOLDED, cap : cap + HD])
            head_copy(h).start()

        return carry

    lax.fori_loop(0, heads, tail_head, 0)

    def start_part(part):
        rows = pl.ds(part * cap, cap)
        part_tx[0, rows] = key_acc[other, rows].astype(jnp.bfloat16)
        part_tx[1, rows] = value_acc[other, rows].astype(jnp.bfloat16)
        part_copy(part).start()

    def finish_part(part):
        rows = pl.ds(part * cap, cap)
        part_copy(part).wait()
        key_grad = (key_acc[sub, rows] + part_rx[0, rows].astype(jnp.float32)) * scaling
        value_grad = value_acc[sub, rows] + part_rx[1, rows].astype(jnp.float32)
        own_kv[0, rows] = key_grad.astype(jnp.bfloat16)
        own_kv[1, rows] = value_grad.astype(jnp.bfloat16)

    start_part(1)

    def top_head(h, carry):
        g = h // per_group
        fetch(0, h, 0).wait()
        fetch(1, h, 0).wait()
        output, query_grad, key_part, value_part, _, _ = attention_rows(
            query_buf[h, :cap], grad_buf[h, :cap], key_buf[g, :cap], value_buf[g, :cap], bias_top[...], scaling
        )
        att_buf[h, :cap] = output
        qg_buf[h, :cap] = query_grad
        key_acc[g, :cap] += key_part
        value_acc[g, :cap] += value_part
        return carry

    lax.fori_loop(0, heads // 2, top_head, 0)
    finish_part(1)

    @pl.when(sender)
    def _():
        kv_tx[...] = own_kv[:, cap:]
        kv_grad_copy().start()

    lax.fori_loop(heads // 2, heads, top_head, 0)
    start_part(0)

    live = jnp.sum(jnp.where(seg >= 0.0, 1, 0), axis=1, keepdims=True)
    live = jnp.sum(live, axis=0, keepdims=True)
    own_moved = handed_ref[me]
    arriving = handed_ref[lax.rem(me, half)]
    kept = jnp.where(sender, length - own_moved, live)
    row = lax.broadcasted_iota(jnp.int32, (length, HD), 0)
    own_row = row < kept

    def out_copy(which, h):
        target = (out_a, out_q)[which]
        source = (att_buf, qg_buf)[which]
        return pltpu.make_async_copy(
            source.at[h], target.at[0, :, columns(h)], out_sem.at[which * heads + h]
        )

    def out_kv(which):
        return pltpu.make_async_copy(own_kv.at[which], (out_k, out_v)[which], out_sem.at[2 * heads + which])

    @pl.when(sender)
    def _():
        def cut_head(h, carry):
            for which, source in enumerate((att_buf, qg_buf)):
                cut = jnp.where(own_row, source[h].astype(jnp.float32), 0.0)
                source[h] = cut.astype(jnp.bfloat16)
                out_copy(which, h).start()
            return carry

        lax.fori_loop(0, heads, cut_head, 0)
        finish_part(0)
        for which in range(2):
            cut = jnp.where(own_row, own_kv[which].astype(jnp.float32), 0.0)
            own_kv[which] = cut.astype(jnp.bfloat16)
            out_kv(which).start()
        kv_copy(0).wait_send()
        kv_copy(1).wait_send()
        kv_grad_copy().wait_send()

        def sent(h, carry):
            head_copy(h).wait_send()
            return carry

        lax.fori_loop(0, heads, sent, 0)

    @pl.when(receiver)
    def _():
        zero_rows = jnp.zeros((HD - FOLDED, HD), jnp.bfloat16)
        for kind in range(2):
            for g in range(groups):
                kv_rx[kind, g, FOLDED:] = zero_rows
        row_of = lax.broadcasted_iota(jnp.int32, (length, cap), 0)
        slot = lax.broadcasted_iota(jnp.int32, (length, cap), 1)
        taken = jnp.logical_and(row_of >= kept, slot == row_of - kept + (cap - arriving))
        perm[...] = jnp.where(taken, 1.0, 0.0).astype(jnp.bfloat16)
        for kind in range(2):
            kv_copy(kind).wait_recv()
            kv_forward(kind).start()
        finish_part(0)
        for kind in range(2):
            kv_forward(kind).wait()

        def place_head(h, carry):
            g = h // per_group
            head_copy(h).wait_recv()
            probs, score_grad = unfolded_rows(rx[h, 2 * rest :])
            output = dot_nn(probs, kv_rx[1, g]).astype(jnp.bfloat16)
            query_grad = (dot_nn(score_grad, kv_rx[0, g]) * scaling).astype(jnp.bfloat16)
            arrived = jnp.concatenate(
                [
                    jnp.concatenate([output, rx[h, :rest]], axis=0),
                    jnp.concatenate([query_grad, rx[h, rest : 2 * rest]], axis=0),
                ],
                axis=1,
            )
            moved = dot_nn(perm[...], arrived)
            for which, source in enumerate((att_buf, qg_buf)):
                placed = jnp.where(own_row, source[h].astype(jnp.float32), moved[:, which * HD : (which + 1) * HD])
                source[h] = placed.astype(jnp.bfloat16)
                out_copy(which, h).start()
            return carry

        lax.fori_loop(0, heads, place_head, 0)
        kv_grad_copy().wait_recv()
        for which in range(2):
            moved = dot_nn(perm[...], kv_grad_rx[which])
            placed = jnp.where(own_row, own_kv[which].astype(jnp.float32), moved)
            own_kv[which] = placed.astype(jnp.bfloat16)
            out_kv(which).start()

    def written(h, carry):
        out_copy(0, h).wait()
        out_copy(1, h).wait()
        return carry

    lax.fori_loop(0, heads, written, 0)
    out_kv(0).wait()
    out_kv(1).wait()


def on_device(n_dp, queries, key_states, value_states, out_grad, seg_ids, handed):
    length = seg_ids.shape[0]
    cap = length // 2
    width = queries.shape[2]
    heads, groups = width // HD, key_states.shape[1] // HD
    kv_width = key_states.shape[1] // 2
    packed = 2 * (cap - FOLDED) + FOLDED
    bf16, f32 = jnp.bfloat16, jnp.float32
    dma = pltpu.SemaphoreType.DMA
    anywhere = pl.BlockSpec(memory_space=pl.ANY)
    return pl.pallas_call(
        functools.partial(kernel, n_dp),
        out_shape=(
            jax.ShapeDtypeStruct(queries.shape, bf16),
            jax.ShapeDtypeStruct(queries.shape, bf16),
            jax.ShapeDtypeStruct((length, kv_width), bf16),
            jax.ShapeDtypeStruct((length, kv_width), bf16),
        ),
        in_specs=[anywhere] * 4
        + [pl.BlockSpec(memory_space=pltpu.VMEM), pl.BlockSpec(memory_space=pltpu.SMEM)],
        out_specs=(anywhere,) * 4,
        scratch_shapes=[
            pltpu.VMEM((heads, length, HD), bf16),
            pltpu.VMEM((heads, length, HD), bf16),
            pltpu.VMEM((groups, length, HD), bf16),
            pltpu.VMEM((groups, length, HD), bf16),
            pltpu.VMEM((heads, length, HD), bf16),
            pltpu.VMEM((heads, length, HD), bf16),
            pltpu.VMEM((cap, cap), f32),
            pltpu.VMEM((cap, length), f32),
            pltpu.VMEM((groups, length, HD), f32),
            pltpu.VMEM((groups, length, HD), f32),
            pltpu.VMEM((length, cap), bf16),
            pltpu.VMEM((heads, packed, HD), bf16),
            pltpu.VMEM((heads, packed, HD), bf16),
            pltpu.VMEM((2, groups, HD, HD), bf16),
            pltpu.VMEM((2, length, HD), bf16),
            pltpu.VMEM((2, length, HD), bf16),
            pltpu.VMEM((2, length, HD), bf16),
            pltpu.VMEM((2, cap, HD), bf16),
            pltpu.VMEM((2, cap, HD), bf16),
            dma((4 * heads + 2 * groups,)),
            dma((2 * heads + 2,)),
            dma((heads,)),
            dma((heads,)),
            dma((2,)),
            dma((2,)),
            dma((2,)),
            dma((2,)),
            dma((2,)),
            dma((2,)),
            dma((1,)),
            dma((1,)),
        ],
        compiler_params=pltpu.CompilerParams(
            collective_id=0, has_side_effects=True, vmem_limit_bytes=40 * 2**20
        ),
    )(queries, key_states, value_states, out_grad, seg_ids.reshape(-1, HD), handed)


def solution(mesh):
    return jax.shard_map(
        functools.partial(on_device, mesh.shape["dp"]),
        mesh=mesh,
        in_specs=(
            P("sub", "dp", "head"),
            P("dp", "head"),
            P("dp", "head"),
            P("sub", "dp", "head"),
            P("dp"),
            P(),
        ),
        out_specs=(
            P("sub", "dp", "head"),
            P("sub", "dp", "head"),
            P("dp", ("head", "sub")),
            P("dp", ("head", "sub")),
        ),
        check_vma=False,
    )
```

time: 169 us -> 63.6 us (0.38)
  the two profiles are of different devices: /device:TPU:1 before, /device:TPU:756 now
where the time goes in v1:
time: 63.6 us; the launch traced here: 63.3 us
  Pallas kernels  53.7 us (84%)
  local copies, waits for them, and re-layouts  8.93 us (14%)
  between operations  0.66 us (1%)
    pallas_call x1, Pallas kernels, on_device(): pl.pallas_call(functools.partial(kernel, n_dp), out_shape=(jax.ShapeDtype...  53.7 us
    unnamed x16, local copies, waits for them, and re-layouts  8.93 us

profile of v1, /device:TPU:756, one launch (start us, length us, event | category | flops | bytes accessed | tf_op | source)
XLA Modules:
  0.0 63.3 jit_solution(487331207831892425)
XLA Ops:
  0.6 0.0 copy-start.5
  0.6 0.6 %copy-done.5 = s32[96]{0:T(128)S(1)} copy-done((s32[96]{0:T(128)S(1)}, s32[96]{0:T(128)}, u32[]{:S(2)}) %copy-start.5) | copy-done | bytes 408
  1.3 0.0 copy-start
  1.3 1.2 %copy-done = bf16[1,512,1024]{2,1,0:T(8,128)(2,1)S(1)} copy-done((bf16[1,512,1024]{2,1,0:T(8,128)(2,1)S(1)}, bf16[1,512,1024]{2,1,0:T(8,128)(2,1)}, u32[]{:S(2)}) %copy-start) | copy-done | bytes 1048600
  2.5 0.0 copy-start.1
  2.5 1.2 %copy-done.1 = bf16[1,512,1024]{2,1,0:T(8,128)(2,1)S(1)} copy-done((bf16[1,512,1024]{2,1,0:T(8,128)(2,1)S(1)}, bf16[1,512,1024]{2,1,0:T(8,128)(2,1)}, u32[]{:S(2)}) %copy-start.1) | copy-done | bytes 1048600
  3.7 0.0 copy-start.2
  3.7 0.9 %copy-done.2 = bf16[512,256]{1,0:T(8,128)(2,1)S(1)} copy-done((bf16[512,256]{1,0:T(8,128)(2,1)S(1)}, bf16[512,256]{1,0:T(8,128)(2,1)}, u32[]{:S(2)}) %copy-start.2) | copy-done | bytes 262168
  4.7 0.0 copy-start.3
  4.7 0.9 %copy-done.3 = bf16[512,256]{1,0:T(8,128)(2,1)S(1)} copy-done((bf16[512,256]{1,0:T(8,128)(2,1)S(1)}, bf16[512,256]{1,0:T(8,128)(2,1)}, u32[]{:S(2)}) %copy-start.3) | copy-done | bytes 262168
  5.6 0.0 copy-start.4
  5.6 0.7 %copy-done.4 = s32[512]{0:T(512)S(1)} copy-done((s32[512]{0:T(512)S(1)}, s32[512]{0:T(512)}, u32[]{:S(2)}) %copy-start.4) | copy-done | bytes 2072
  6.3 53.7 %shard_map.93 = (bf16[1,512,1024]{2,1,0:T(8,128)(2,1)S(1)}, bf16[1,512,1024]{2,1,0:T(8,128)(2,1)S(1)}, bf16[512,128]{1,0:T(8,128)(2,1)S(1)}, bf16[512,128]{1,0:T(8,128)(2,1)S(1)}) custom-call(bf16[1,512,1024]{2,1,0:T(8,128)(2,1)S(1)} %copy-done, bf16[512,256]{1,0:T(8,128)(2,1)S(1)} %copy-done.2, bf16[512,256]{1,0:T(8,128)(2,1)S(1)} %copy-done.3, ...), custom_call_target="tpu_custom_call" | custom-call | tf_op jit(solution)/shard_map/pallas_call | solution.py:367
  60.1 1.0 %copy.14 = bf16[1,512,1024]{2,1,0:T(8,128)(2,1)} copy(bf16[1,512,1024]{2,1,0:T(8,128)(2,1)S(1)} %get-tuple-element.8) | data formatting | bytes 2097152
  61.0 1.0 %copy.15 = bf16[1,512,1024]{2,1,0:T(8,128)(2,1)} copy(bf16[1,512,1024]{2,1,0:T(8,128)(2,1)S(1)} %get-tuple-element.9) | data formatting | bytes 2097152
  62.0 0.7 %copy.16 = bf16[512,128]{1,0:T(8,128)(2,1)} copy(bf16[512,128]{1,0:T(8,128)(2,1)S(1)} %get-tuple-element.10) | data formatting | bytes 262144
  62.7 0.7 %copy.17 = bf16[512,128]{1,0:T(8,128)(2,1)} copy(bf16[512,128]{1,0:T(8,128)(2,1)S(1)} %get-tuple-element.11) | data formatting | bytes 262144
Async XLA Ops:
  0.6 0.7 %copy-start.5 = (s32[96]{0:T(128)S(1)}, s32[96]{0:T(128)}, u32[]{:S(2)}) copy-start(s32[96]{0:T(128)} %handed_ref.1) | copy-start | bytes 1156
  1.3 1.2 %copy-start = (bf16[1,512,1024]{2,1,0:T(8,128)(2,1)S(1)}, bf16[1,512,1024]{2,1,0:T(8,128)(2,1)}, u32[]{:S(2)}) copy-start(bf16[1,512,1024]{2,1,0:T(8,128)(2,1)} %query_in.1) | copy-start | bytes 3145732
  2.5 1.2 %copy-start.1 = (bf16[1,512,1024]{2,1,0:T(8,128)(2,1)S(1)}, bf16[1,512,1024]{2,1,0:T(8,128)(2,1)}, u32[]{:S(2)}) copy-start(bf16[1,512,1024]{2,1,0:T(8,128)(2,1)} %grad_in.1) | copy-start | bytes 3145732
  3.7 0.9 %copy-start.2 = (bf16[512,256]{1,0:T(8,128)(2,1)S(1)}, bf16[512,256]{1,0:T(8,128)(2,1)}, u32[]{:S(2)}) copy-start(bf16[512,256]{1,0:T(8,128)(2,1)} %key_in.1) | copy-start | bytes 786436
  4.7 0.9 %copy-start.3 = (bf16[512,256]{1,0:T(8,128)(2,1)S(1)}, bf16[512,256]{1,0:T(8,128)(2,1)}, u32[]{:S(2)}) copy-start(bf16[512,256]{1,0:T(8,128)(2,1)} %value_in.1) | copy-start | bytes 786436
  5.6 0.7 %copy-start.4 = (s32[512]{0:T(512)S(1)}, s32[512]{0:T(512)}, u32[]{:S(2)}) copy-start(s32[512]{0:T(512)} %param.10) | copy-start | bytes 6148

commit v2 on v1

--- a/solution.py
+++ b/solution.py
@@ -10,6 +10,7 @@
 HD = 128
 STEP = 16
 PAIRS = 3
+PIECES = 4
 FOLDED = STEP * (2 * PAIRS + 1)
 LOG2_E = 1.4426950408889634
 MASKED = -1e30
@@ -74,11 +75,11 @@
 
 def kernel(
     n_dp,
-    query_in, key_in, value_in, grad_in, seg_ref, handed_ref,
+    query_in, key_in, value_in, grad_in, seg_in, handed_in,
     out_a, out_q, out_k, out_v,
-    query_buf, grad_buf, key_buf, value_buf, att_buf, qg_buf, bias_top, bias_tail,
+    seg_ref, handed_ref, query_buf, grad_buf, key_buf, value_buf, att_buf, qg_buf, bias_top, bias_tail,
     key_acc, value_acc, perm, tx, rx, kv_rx, part_tx, part_rx, own_kv, kv_tx, kv_grad_rx,
-    in_sem, out_sem, tx_send, tx_recv, kv_send, kv_recv, fwd_send, fwd_recv,
+    small_sem, in_sem, out_sem, tx_send, tx_recv, kv_send, kv_recv, fwd_send, fwd_recv,
     part_send, part_recv, kvg_send, kvg_recv,
 ):
     length, width = query_in.shape[1], query_in.shape[2]
@@ -145,9 +146,13 @@
     def kv_grad_copy():
         return remote(kv_tx, kv_grad_rx, kvg_send.at[0], kvg_recv.at[0], partner)
 
+    fetch_seg = pltpu.make_async_copy(seg_in, seg_ref, small_sem.at[0])
+    fetch_handed = pltpu.make_async_copy(handed_in, handed_ref, small_sem.at[1])
+    fetch_seg.start()
     for g in range(groups):
         fetch_kv(0, g).start()
         fetch_kv(1, g).start()
+    fetch_handed.start()
     for part in (1, 0):
         for h in range(heads):
             fetch(0, h, part).start()
@@ -156,16 +161,7 @@
     barrier = pltpu.get_barrier_semaphore()
     pl.semaphore_signal(barrier, inc=1, device_id=partner, device_id_type=MESH)
     pl.semaphore_signal(barrier, inc=1, device_id=twin, device_id_type=MESH)
-    for g in range(groups):
-        fetch_kv(0, g).wait()
-        fetch_kv(1, g).wait()
-    pl.semaphore_wait(barrier, 2)
-
-    @pl.when(sender)
-    def _():
-        kv_copy(0).start()
-        kv_copy(1).start()
-
+    fetch_seg.wait()
     seg = seg_ref[...].astype(jnp.float32)
     square = (HD, HD)
     below = lax.broadcasted_iota(jnp.int32, square, 1) <= lax.broadcasted_iota(jnp.int32, square, 0)
@@ -190,8 +186,11 @@
                 bias_tail[begin : begin + HD, b * HD : (b + 1) * HD] = tile
     key_acc[...] = jnp.zeros_like(key_acc)
     value_acc[...] = jnp.zeros_like(value_acc)
-
-    def tail_head(h, carry):
+    for g in range(groups):
+        fetch_kv(0, g).wait()
+        fetch_kv(1, g).wait()
+
+    def tail_head(h):
         g = h // per_group
         fetch(0, h, 1).wait()
         fetch(1, h, 1).wait()
@@ -210,11 +209,26 @@
             tx[h, :rest] = output[FOLDED:]
             tx[h, rest : 2 * rest] = query_grad[FOLDED:]
             tx[h, 2 * rest :] = folded_rows(probs[:FOLDED, cap : cap + HD], score_grad[:FOLDED, cap : cap + HD])
+
+    def sent_head(h, carry):
+        tail_head(h)
+
+        @pl.when(sender)
+        def _():
             head_copy(h).start()
 
         return carry
 
-    lax.fori_loop(0, heads, tail_head, 0)
+    tail_head(0)
+    pl.semaphore_wait(barrier, 2)
+
+    @pl.when(sender)
+    def _():
+        kv_copy(0).start()
+        kv_copy(1).start()
+        head_copy(0).start()
+
+    lax.fori_loop(1, heads, sent_head, 0)
 
     def start_part(part):
         rows = pl.ds(part * cap, cap)
@@ -258,6 +272,7 @@
 
     live = jnp.sum(jnp.where(seg >= 0.0, 1, 0), axis=1, keepdims=True)
     live = jnp.sum(live, axis=0, keepdims=True)
+    fetch_handed.wait()
     own_moved = handed_ref[me]
     arriving = handed_ref[lax.rem(me, half)]
     kept = jnp.where(sender, length - own_moved, live)
@@ -354,6 +369,26 @@
     out_kv(1).wait()
 
 
+def write_kernel(att, query_grad, key_grad, value_grad, out_a, out_q, out_k, out_v, rows_buf, kv_buf, read, write):
+    step = att.shape[1] // PIECES
+    moves = []
+    for which, (source, target) in enumerate(((att, out_a), (query_grad, out_q))):
+        for piece in range(PIECES):
+            rows = pl.ds(piece * step, step)
+            moves.append((source.at[:, rows], rows_buf.at[pl.ds(which, 1), rows], target.at[:, rows]))
+    moves.append((key_grad, kv_buf.at[0], out_k))
+    moves.append((value_grad, kv_buf.at[1], out_v))
+    reads = [pltpu.make_async_copy(a, b, read.at[i]) for i, (a, b, c) in enumerate(moves)]
+    writes = [pltpu.make_async_copy(b, c, write.at[i]) for i, (a, b, c) in enumerate(moves)]
+    for copy in reads:
+        copy.start()
+    for arrived, copy in zip(reads, writes):
+        arrived.wait()
+        copy.start()
+    for copy in writes:
+        copy.wait()
+
+
 def on_device(n_dp, queries, key_states, value_states, out_grad, seg_ids, handed):
     length = seg_ids.shape[0]
     cap = length // 2
@@ -364,18 +399,20 @@
     bf16, f32 = jnp.bfloat16, jnp.float32
     dma = pltpu.SemaphoreType.DMA
     anywhere = pl.BlockSpec(memory_space=pl.ANY)
-    return pl.pallas_call(
+    results = (
+        jax.ShapeDtypeStruct(queries.shape, bf16),
+        jax.ShapeDtypeStruct(queries.shape, bf16),
+        jax.ShapeDtypeStruct((length, kv_width), bf16),
+        jax.ShapeDtypeStruct((length, kv_width), bf16),
+    )
+    placed = pl.pallas_call(
         functools.partial(kernel, n_dp),
-        out_shape=(
-            jax.ShapeDtypeStruct(queries.shape, bf16),
-            jax.ShapeDtypeStruct(queries.shape, bf16),
-            jax.ShapeDtypeStruct((length, kv_width), bf16),
-            jax.ShapeDtypeStruct((length, kv_width), bf16),
-        ),
-        in_specs=[anywhere] * 4
-        + [pl.BlockSpec(memory_space=pltpu.VMEM), pl.BlockSpec(memory_space=pltpu.SMEM)],
+        out_shape=results,
+        in_specs=[anywhere] * 6,
         out_specs=(anywhere,) * 4,
         scratch_shapes=[
+            pltpu.VMEM((length // HD, HD), jnp.int32),
+            pltpu.SMEM(handed.shape, jnp.int32),
             pltpu.VMEM((heads, length, HD), bf16),
             pltpu.VMEM((heads, length, HD), bf16),
             pltpu.VMEM((groups, length, HD), bf16),
@@ -395,6 +432,7 @@
             pltpu.VMEM((2, length, HD), bf16),
             pltpu.VMEM((2, cap, HD), bf16),
             pltpu.VMEM((2, cap, HD), bf16),
+            dma((2,)),
             dma((4 * heads + 2 * groups,)),
             dma((2 * heads + 2,)),
             dma((heads,)),
@@ -409,9 +447,22 @@
             dma((1,)),
         ],
         compiler_params=pltpu.CompilerParams(
-            collective_id=0, has_side_effects=True, vmem_limit_bytes=40 * 2**20
+            collective_id=0, has_side_effects=True, vmem_limit_bytes=63 * 2**20
         ),
     )(queries, key_states, value_states, out_grad, seg_ids.reshape(-1, HD), handed)
+    return pl.pallas_call(
+        write_kernel,
+        out_shape=results,
+        in_specs=[anywhere] * 4,
+        out_specs=(anywhere,) * 4,
+        scratch_shapes=[
+            pltpu.VMEM((2, length, width), bf16),
+            pltpu.VMEM((2, length, kv_width), bf16),
+            dma((2 * PIECES + 2,)),
+            dma((2 * PIECES + 2,)),
+        ],
+        compiler_params=pltpu.CompilerParams(vmem_limit_bytes=63 * 2**20),
+    )(*placed)
 
 
 def solution(mesh):

time: 63.6 us -> 55.5 us (0.87)
  local copies, waits for them, and re-layouts: 8.93 us -> 0 us
  Pallas kernels: 53.7 us -> 54.6 us
    unnamed x16 -> x0, local copies, waits for them, and re-layouts: 8.93 us -> none
    pallas_call x1 -> x2, Pallas kernels: 53.7 us -> 54.6 us  [the longest x1 52.1 us: on_device(): pl.pallas_call(functools.partial(kernel, n_dp), out_shape=results, in_spe...]
where the time goes in v2:
time: 55.5 us; the launch traced here: 55.3 us
  Pallas kernels  54.6 us (98%)
  between operations  0.64 us (1%)
    pallas_call x1, Pallas kernels, on_device(): pl.pallas_call(functools.partial(kernel, n_dp), out_shape=results, in_spe...  52.1 us
    pallas_call x1, Pallas kernels, on_device(): pl.pallas_call(write_kernel, out_shape=results, in_specs=[anywhere] * 4,...  2.51 us

profile of v2, /device:TPU:756, one launch (start us, length us, event | category | flops | bytes accessed | tf_op | source)
XLA Modules:
  0.0 55.3 jit_solution(863497397294896685)
XLA Ops:
  0.6 52.1 %shard_map.93 = (bf16[1,512,1024]{2,1,0:T(8,128)(2,1)}, bf16[1,512,1024]{2,1,0:T(8,128)(2,1)}, bf16[512,128]{1,0:T(8,128)(2,1)}, bf16[512,128]{1,0:T(8,128)(2,1)}) custom-call(bf16[1,512,1024]{2,1,0:T(8,128)(2,1)} %query_in.1, bf16[512,256]{1,0:T(8,128)(2,1)} %key_in.1, bf16[512,256]{1,0:T(8,128)(2,1)} %value_in.1, bf16[1,512,1024]{2,1,0:T(8,128)(2,1)} %grad_in.1, ...), custom_call_target="tpu_custom_call" | custom-call | tf_op jit(solution)/shard_map/pallas_call | solution.py:408
  52.7 2.5 %shard_map.94 = (bf16[1,512,1024]{2,1,0:T(8,128)(2,1)}, bf16[1,512,1024]{2,1,0:T(8,128)(2,1)}, bf16[512,128]{1,0:T(8,128)(2,1)}, bf16[512,128]{1,0:T(8,128)(2,1)}) custom-call(bf16[1,512,1024]{2,1,0:T(8,128)(2,1)} %get-tuple-element.8.att, bf16[1,512,1024]{2,1,0:T(8,128)(2,1)} %get-tuple-element.9.query_grad, bf16[512,128]{1,0:T(8,128)(2,1)} %get-tuple-element.10.key_grad, ...), custom_call_target="tpu_custom_call" | custom-call | tf_op jit(solution)/shard_map/pallas_call | solution.py:453

commit v3 on v2

--- a/solution.py
+++ b/solution.py
@@ -8,10 +8,8 @@
 from jax.sharding import PartitionSpec as P
 
 HD = 128
-STEP = 16
-PAIRS = 3
 PIECES = 4
-FOLDED = STEP * (2 * PAIRS + 1)
+FOLDED = HD
 LOG2_E = 1.4426950408889634
 MASKED = -1e30
 MESH = pl.DeviceIdType.MESH
@@ -42,34 +40,37 @@
     return output, query_grad, dot_tn(rounded, query), dot_tn(weights, grad), probs, score_grad
 
 
+def reversal(rows):
+    row = lax.broadcasted_iota(jnp.int32, (rows, rows), 0)
+    column = lax.broadcasted_iota(jnp.int32, (rows, rows), 1)
+    return jnp.where(row + column == rows - 1, 1.0, 0.0).astype(jnp.bfloat16)
+
+
 def folded_rows(probs, score_grad):
-    rows = []
+    half = HD // 2
+    row = lax.broadcasted_iota(jnp.int32, (half, HD), 0)
+    lane = lax.broadcasted_iota(jnp.int32, (half, HD), 1)
+    packed = []
     for square in (probs, score_grad):
-        for j in range(PAIRS):
-            low = square[STEP * j : STEP * (j + 1)]
-            high = square[STEP * (2 * PAIRS - j) : STEP * (2 * PAIRS - j + 1)]
-            rows.append(low + pltpu.roll(high, STEP * (j + 1), 1))
-    middle = slice(STEP * PAIRS, STEP * (PAIRS + 1))
-    rows.append(probs[middle] + pltpu.roll(score_grad[middle], HD // 2, 1))
-    return jnp.concatenate(rows, axis=0).astype(jnp.bfloat16)
+        upper = jnp.where(lane < row, square[:half], 0.0).astype(jnp.bfloat16)
+        turned = pltpu.roll(dot_nn(reversal(half), upper), half + 1, 1, stride=1, stride_axis=0)
+        packed.append(square[half:] + turned)
+    return jnp.concatenate(packed, axis=0).astype(jnp.bfloat16)
 
 
 def unfolded_rows(packed):
-    packed = packed.astype(jnp.float32)
-    lane = lax.broadcasted_iota(jnp.int32, (STEP, HD), 1)
-    last = packed[2 * PAIRS * STEP :]
+    half = HD // 2
+    row = lax.broadcasted_iota(jnp.int32, (half, HD), 0)
+    lane = lax.broadcasted_iota(jnp.int32, (half, HD), 1)
     squares = []
-    for which in range(2):
-        low, high = [], []
-        for j in range(PAIRS):
-            start = (which * PAIRS + j) * STEP
-            rows = packed[start : start + STEP]
-            low.append(jnp.where(lane < STEP * (j + 1), rows, 0.0))
-            turned = pltpu.roll(rows, HD - STEP * (j + 1), 1)
-            high.append(jnp.where(lane < STEP * (2 * PAIRS + 1 - j), turned, 0.0))
-        turned = pltpu.roll(last, HD // 2, 1) if which else last
-        middle = jnp.where(lane < HD // 2, turned, 0.0)
-        squares.append(jnp.concatenate(low + [middle] + high[::-1], axis=0).astype(jnp.bfloat16))
+    for which, total in enumerate((1.0, 0.0)):
+        rows = packed[which * half : (which + 1) * half].astype(jnp.float32)
+        lower = jnp.where(lane <= row + half, rows, 0.0)
+        rest = jnp.where(lane <= row + half, 0.0, rows).astype(jnp.bfloat16)
+        upper = pltpu.roll(dot_nn(reversal(half), rest), 0, 1, stride=1, stride_axis=0)
+        diagonal = total - jnp.sum(upper, axis=1, keepdims=True)
+        upper = jnp.where(lane == row, diagonal, upper)
+        squares.append(jnp.concatenate([upper, lower], axis=0).astype(jnp.bfloat16))
     return squares
 
 
@@ -316,10 +317,6 @@
 
     @pl.when(receiver)
     def _():
-        zero_rows = jnp.zeros((HD - FOLDED, HD), jnp.bfloat16)
-        for kind in range(2):
-            for g in range(groups):
-                kv_rx[kind, g, FOLDED:] = zero_rows
         row_of = lax.broadcasted_iota(jnp.int32, (length, cap), 0)
         slot = lax.broadcasted_iota(jnp.int32, (length, cap), 1)
         taken = jnp.logical_and(row_of >= kept, slot == row_of - kept + (cap - arriving))

time: 55.5 us -> 54.4 us (0.980)
  the two profiles are of different devices: /device:TPU:756 before, /device:TPU:752 now
where the time goes in v3:
time: 54.4 us; the launch traced here: 54.2 us
  Pallas kernels  53.6 us (99%)
  between operations  0.64 us (1%)
    pallas_call x1, Pallas kernels, on_device(): pl.pallas_call(functools.partial(kernel, n_dp), out_shape=results, in_spe...  51.1 us
    pallas_call x1, Pallas kernels, on_device(): pl.pallas_call(write_kernel, out_shape=results, in_specs=[anywhere] * 4,...  2.51 us

profile of v3, /device:TPU:752, one launch (start us, length us, event | category | flops | bytes accessed | tf_op | source)
XLA Modules:
  0.0 54.2 jit_solution(7869661941284913040)
XLA Ops:
  0.6 51.1 %shard_map.93 = (bf16[1,512,1024]{2,1,0:T(8,128)(2,1)}, bf16[1,512,1024]{2,1,0:T(8,128)(2,1)}, bf16[512,128]{1,0:T(8,128)(2,1)}, bf16[512,128]{1,0:T(8,128)(2,1)}) custom-call(bf16[1,512,1024]{2,1,0:T(8,128)(2,1)} %query_in.1, bf16[512,256]{1,0:T(8,128)(2,1)} %key_in.1, bf16[512,256]{1,0:T(8,128)(2,1)} %value_in.1, bf16[1,512,1024]{2,1,0:T(8,128)(2,1)} %grad_in.1, ...), custom_call_target="tpu_custom_call" | custom-call | tf_op jit(solution)/shard_map/pallas_call | solution.py:405
  51.7 2.5 %shard_map.94 = (bf16[1,512,1024]{2,1,0:T(8,128)(2,1)}, bf16[1,512,1024]{2,1,0:T(8,128)(2,1)}, bf16[512,128]{1,0:T(8,128)(2,1)}, bf16[512,128]{1,0:T(8,128)(2,1)}) custom-call(bf16[1,512,1024]{2,1,0:T(8,128)(2,1)} %get-tuple-element.8.att, bf16[1,512,1024]{2,1,0:T(8,128)(2,1)} %get-tuple-element.9.query_grad, bf16[512,128]{1,0:T(8,128)(2,1)} %get-tuple-element.10.key_grad, ...), custom_call_target="tpu_custom_call" | custom-call | tf_op jit(solution)/shard_map/pallas_call | solution.py:450

commit v4 on v3

--- a/solution.py
+++ b/solution.py
@@ -77,9 +77,9 @@
 def kernel(
     n_dp,
     query_in, key_in, value_in, grad_in, seg_in, handed_in,
-    out_a, out_q, out_k, out_v,
+    out_a, out_q, out_kv, out_perm, kv_grad_rx,
     seg_ref, handed_ref, query_buf, grad_buf, key_buf, value_buf, att_buf, qg_buf, bias_top, bias_tail,
-    key_acc, value_acc, perm, tx, rx, kv_rx, part_tx, part_rx, own_kv, kv_tx, kv_grad_rx,
+    key_acc, value_acc, perm, tx, rx, kv_rx, part_tx, part_rx, own_kv, kv_tx,
     small_sem, in_sem, out_sem, tx_send, tx_recv, kv_send, kv_recv, fwd_send, fwd_recv,
     part_send, part_recv, kvg_send, kvg_recv,
 ):
@@ -287,8 +287,15 @@
             source.at[h], target.at[0, :, columns(h)], out_sem.at[which * heads + h]
         )
 
-    def out_kv(which):
-        return pltpu.make_async_copy(own_kv.at[which], (out_k, out_v)[which], out_sem.at[2 * heads + which])
+    def finish_kv():
+        finish_part(0)
+        for which in range(2):
+            cut = jnp.where(own_row, own_kv[which].astype(jnp.float32), 0.0)
+            own_kv[which] = cut.astype(jnp.bfloat16)
+        keep_kv.start()
+
+    keep_kv = pltpu.make_async_copy(own_kv, out_kv, out_sem.at[2 * heads])
+    keep_perm = pltpu.make_async_copy(perm, out_perm, out_sem.at[2 * heads + 1])
 
     @pl.when(sender)
     def _():
@@ -300,11 +307,7 @@
             return carry
 
         lax.fori_loop(0, heads, cut_head, 0)
-        finish_part(0)
-        for which in range(2):
-            cut = jnp.where(own_row, own_kv[which].astype(jnp.float32), 0.0)
-            own_kv[which] = cut.astype(jnp.bfloat16)
-            out_kv(which).start()
+        finish_kv()
         kv_copy(0).wait_send()
         kv_copy(1).wait_send()
         kv_grad_copy().wait_send()
@@ -321,10 +324,11 @@
         slot = lax.broadcasted_iota(jnp.int32, (length, cap), 1)
         taken = jnp.logical_and(row_of >= kept, slot == row_of - kept + (cap - arriving))
         perm[...] = jnp.where(taken, 1.0, 0.0).astype(jnp.bfloat16)
+        keep_perm.start()
         for kind in range(2):
             kv_copy(kind).wait_recv()
             kv_forward(kind).start()
-        finish_part(0)
+        finish_kv()
         for kind in range(2):
             kv_forward(kind).wait()
 
@@ -349,12 +353,7 @@
             return carry
 
         lax.fori_loop(0, heads, place_head, 0)
-        kv_grad_copy().wait_recv()
-        for which in range(2):
-            moved = dot_nn(perm[...], kv_grad_rx[which])
-            placed = jnp.where(own_row, own_kv[which].astype(jnp.float32), moved)
-            own_kv[which] = placed.astype(jnp.bfloat16)
-            out_kv(which).start()
+        keep_perm.wait()
 
     def written(h, carry):
         out_copy(0, h).wait()
@@ -362,25 +361,54 @@
         return carry
 
     lax.fori_loop(0, heads, written, 0)
-    out_kv(0).wait()
-    out_kv(1).wait()
-
-
-def write_kernel(att, query_grad, key_grad, value_grad, out_a, out_q, out_k, out_v, rows_buf, kv_buf, read, write):
+    keep_kv.wait()
+
+    @pl.when(receiver)
+    def _():
+        kv_grad_copy().wait_recv()
+
+
+def write_kernel(
+    n_dp, att, query_grad, own_kv, perm, arrived, out_a, out_q, out_k, out_v,
+    rows_buf, kv_buf, perm_buf, arrived_buf, read, write,
+):
+    receiver = lax.axis_index("dp") >= n_dp // 2
     step = att.shape[1] // PIECES
     moves = []
     for which, (source, target) in enumerate(((att, out_a), (query_grad, out_q))):
         for piece in range(PIECES):
             rows = pl.ds(piece * step, step)
             moves.append((source.at[:, rows], rows_buf.at[pl.ds(which, 1), rows], target.at[:, rows]))
-    moves.append((key_grad, kv_buf.at[0], out_k))
-    moves.append((value_grad, kv_buf.at[1], out_v))
     reads = [pltpu.make_async_copy(a, b, read.at[i]) for i, (a, b, c) in enumerate(moves)]
     writes = [pltpu.make_async_copy(b, c, write.at[i]) for i, (a, b, c) in enumerate(moves)]
+    count = len(moves)
+    read_kv = pltpu.make_async_copy(own_kv, kv_buf, read.at[count])
+    read_perm = pltpu.make_async_copy(perm, perm_buf, read.at[count + 1])
+    read_arrived = pltpu.make_async_copy(arrived, arrived_buf, read.at[count + 2])
+
+    @pl.when(receiver)
+    def _():
+        read_perm.start()
+        read_arrived.start()
+
+    read_kv.start()
     for copy in reads:
         copy.start()
-    for arrived, copy in zip(reads, writes):
-        arrived.wait()
+    read_kv.wait()
+
+    @pl.when(receiver)
+    def _():
+        read_perm.wait()
+        read_arrived.wait()
+        for which in range(2):
+            moved = dot_nn(perm_buf[...], arrived_buf[which])
+            kv_buf[which] = (kv_buf[which].astype(jnp.float32) + moved).astype(jnp.bfloat16)
+
+    for which, target in enumerate((out_k, out_v)):
+        writes.append(pltpu.make_async_copy(kv_buf.at[which], target, write.at[count + which]))
+        writes[-1].start()
+    for landed, copy in zip(reads, writes):
+        landed.wait()
         copy.start()
     for copy in writes:
         copy.wait()
@@ -404,9 +432,14 @@
     )
     placed = pl.pallas_call(
         functools.partial(kernel, n_dp),
-        out_shape=results,
+        out_shape=results[:2]
+        + (
+            jax.ShapeDtypeStruct((2, length, HD), bf16),
+            jax.ShapeDtypeStruct((length, cap), bf16),
+            jax.ShapeDtypeStruct((2, cap, HD), bf16),
+        ),
         in_specs=[anywhere] * 6,
-        out_specs=(anywhere,) * 4,
+        out_specs=(anywhere,) * 5,
         scratch_shapes=[
             pltpu.VMEM((length // HD, HD), jnp.int32),
             pltpu.SMEM(handed.shape, jnp.int32),
@@ -428,7 +461,6 @@
             pltpu.VMEM((2, length, HD), bf16),
             pltpu.VMEM((2, length, HD), bf16),
             pltpu.VMEM((2, cap, HD), bf16),
-            pltpu.VMEM((2, cap, HD), bf16),
             dma((2,)),
             dma((4 * heads + 2 * groups,)),
             dma((2 * heads + 2,)),
@@ -448,14 +480,16 @@
         ),
     )(queries, key_states, value_states, out_grad, seg_ids.reshape(-1, HD), handed)
     return pl.pallas_call(
-        write_kernel,
+        functools.partial(write_kernel, n_dp),
         out_shape=results,
-        in_specs=[anywhere] * 4,
+        in_specs=[anywhere] * 5,
         out_specs=(anywhere,) * 4,
         scratch_shapes=[
             pltpu.VMEM((2, length, width), bf16),
-            pltpu.VMEM((2, length, kv_width), bf16),
-            dma((2 * PIECES + 2,)),
+            pltpu.VMEM((2, length, HD), bf16),
+            pltpu.VMEM((length, cap), bf16),
+            pltpu.VMEM((2, cap, HD), bf16),
+            dma((2 * PIECES + 3,)),
             dma((2 * PIECES + 2,)),
         ],
         compiler_params=pltpu.CompilerParams(vmem_limit_bytes=63 * 2**20),

time: 54.4 us -> 54 us (level)
  the two profiles are of different devices: /device:TPU:752 before, /device:TPU:758 now
where the time goes in v4:
time: 54 us; the launch traced here: 53.8 us
  Pallas kernels  53.1 us (98%)
  between operations  0.64 us (1%)
    pallas_call x1, Pallas kernels, on_device(): pl.pallas_call(functools.partial(kernel, n_dp), out_shape=results[:2] + (...  50.1 us
    pallas_call x1, Pallas kernels, on_device(): pl.pallas_call(functools.partial(write_kernel, n_dp), out_shape=results,...  2.99 us

profile of v4, /device:TPU:758, one launch (start us, length us, event | category | flops | bytes accessed | tf_op | source)
XLA Modules:
  0.0 53.8 jit_solution(8488581179442222310)
XLA Ops:
  0.6 50.1 %shard_map.93 = (bf16[1,512,1024]{2,1,0:T(8,128)(2,1)}, bf16[1,512,1024]{2,1,0:T(8,128)(2,1)}, bf16[2,512,128]{2,1,0:T(8,128)(2,1)}, bf16[512,256]{1,0:T(8,128)(2,1)}, bf16[2,256,128]{2,1,0:T(8,128)(2,1)}) custom-call(bf16[1,512,1024]{2,1,0:T(8,128)(2,1)} %query_in.1, bf16[512,256]{1,0:T(8,128)(2,1)} %key_in.1, bf16[512,256]{1,0:T(8,128)(2,1)} %value_in.1, ...), custom_call_target="tpu_custom_call" | custom-call | tf_op jit(solution)/shard_map/pallas_call | solution.py:433
  50.8 3.0 %shard_map.94 = (bf16[1,512,1024]{2,1,0:T(8,128)(2,1)}, bf16[1,512,1024]{2,1,0:T(8,128)(2,1)}, bf16[512,128]{1,0:T(8,128)(2,1)}, bf16[512,128]{1,0:T(8,128)(2,1)}) custom-call(bf16[1,512,1024]{2,1,0:T(8,128)(2,1)} %get-tuple-element.9.att, bf16[1,512,1024]{2,1,0:T(8,128)(2,1)} %get-tuple-element.10.query_grad, ...), custom_call_target="tpu_custom_call" | custom-call | tf_op jit(solution)/shard_map/pallas_call | solution.py:482
